TPU v7x, 256 devices: a whole 4x4x8 slice. The times are simulated.
256 devices in a mesh: dp: 32 (over y, z), fsdp: 8 (over x, core).
Axes of the slice: x: 4, y: 4, z: 8, core: 2. Of those that a mesh axis runs over, the one named last changes fastest.
Arguments:
- mixed_heads: bfloat16 [65536, 4096], P(('dp', 'fsdp')), may hold values from -6 to 6
- out_grads: bfloat16 [65536, 4608], P(('dp', 'fsdp')), may hold values from -60 to 60
- admit_counts: int32 [256], P(('dp', 'fsdp')), may hold values from 1 to 3, as said below
- lengths: int32 [256, 3], P(('dp', 'fsdp')), may hold values from 60 to 80, as said below
- gauss_noise: float32 [4096, 4608], P('dp', 'fsdp'), may hold values from -6000 to 6000
Outputs:
- grad_shard: float32 [4096, 4608], P('dp', 'fsdp')
Inputs may be any that keep to these rules, and one draw needn't show every extreme that they name: `admit_counts`: A device at dp index i admits at most 2 + 2 i // 32 sequences. In every draw the devices of one fsdp index each admit that most, every sequence 80 tokens long, so the devices of one fsdp index together hold at most 6400 admitted tokens and some hold exactly that many. `lengths`: row e gives the token counts of device e's sequences in order; only the first admit_counts[e] entries are admitted, and these fill the first slots of the device's block.
All inputs are finite; a program needn't handle non-finite values.
Results may differ from a plain program's by a relative error of at most 0.00036.
Values may be sent and summed in bfloat16 or wider, within the bound.
A program may use at most 128 MiB of HBM per device.

v0:
```python
import jax
import jax.numpy as jnp
from jax import lax
from jax.sharding import PartitionSpec as P

MAXSEQ = 3
CLIP = 360000


def device_clip(block_in, block_grad, count, seq_lengths):
    act_gram = lax.dot_general(
        block_in, block_in, (((1,), (1,)), ((), ())), preferred_element_type=jnp.float32
    )
    grad_gram = lax.dot_general(
        block_grad, block_grad, (((1,), (1,)), ((), ())), preferred_element_type=jnp.float32
    )
    admitted_seq = jnp.arange(MAXSEQ, dtype=jnp.int32) < count
    used = jnp.where(admitted_seq, seq_lengths, 0)
    ends = jnp.cumsum(used)
    starts = ends - used
    positions = jnp.arange(block_in.shape[0], dtype=jnp.int32)
    member = (
        (positions[None, :] >= starts[:, None]) & (positions[None, :] < ends[:, None])
    ).astype(jnp.float32)
    product = act_gram * grad_gram
    spread = jnp.dot(member, product, precision=lax.Precision.HIGHEST)
    norm_sq = jnp.sum(spread * member, axis=1)
    factor = CLIP / jnp.maximum(jnp.sqrt(norm_sq), jnp.float32(CLIP))
    row_factor = jnp.sum(member * factor[:, None], axis=0)
    clipped = (row_factor[:, None] * block_grad.astype(jnp.float32)).astype(jnp.bfloat16)
    return (clipped, jnp.sum(used))


def on_device(mixed_heads, out_grads, admit_counts, lengths, gauss_noise):
    clipped, live_rows = device_clip(mixed_heads, out_grads, admit_counts[0], lengths[0])
    grad_cols = lax.all_to_all(clipped, "fsdp", split_axis=1, concat_axis=0, tiled=True)
    partial_grad = lax.dot_general(
        lax.all_gather(mixed_heads, "fsdp", axis=0, tiled=True),
        grad_cols,
        (((0,), (0,)), ((), ())),
        preferred_element_type=jnp.float32,
    )
    owned = lax.psum_scatter(partial_grad, "dp", scatter_dimension=0, tiled=True)
    admitted = lax.psum(admit_counts[0], ("dp", "fsdp"))
    return (owned + gauss_noise) / admitted.astype(jnp.float32)


def solution(mesh):
    in_specs = (
        P(("dp", "fsdp"), None),
        P(("dp", "fsdp"), None),
        P(("dp", "fsdp")),
        P(("dp", "fsdp"), None),
        P("dp", "fsdp"),
    )
    out_specs = P("dp", "fsdp")
    return jax.shard_map(
        on_device, mesh=mesh, in_specs=in_specs, out_specs=out_specs, check_vma=False
    )
```

profile of v0, /device:TPU:1, one launch (start us, length us, event | category | flops | bytes accessed | tf_op | source)
XLA Modules:
  0.0 375.1 jit_solution(4648600792313618319)
XLA Ops:
  6.5 0.0 all-gather.2.cloned.1.call-start
  6.5 0.7 all-gather.2.cloned.1.call-update
  7.3 0.0 reduce-scatter.2.cloned.1.call-start
  7.9 0.0 copy-start.3
  8.0 4.3 %copy.6 = bf16[256,4608]{0,1:T(8,128)(2,1)} copy(bf16[256,4608]{1,0:T(8,128)(2,1)} %param.6) | data formatting | bytes 4718592 | tf_op args[1]
  12.2 0.0 copy-done.3
  12.2 0.2 reduce-window.7
  12.4 3.1 fusion.4
  15.5 0.0 copy-done
  15.5 0.0 copy-start.1
  15.5 0.8 convolution_multiply_fusion
  16.3 0.3 fusion
  16.7 0.1 select_reduce_fusion
  16.8 0.4 copy-done.1
  17.2 0.5 multiply_convert_fusion
  17.7 56.0 %all_to_all.19 = bf16[256,8,576]{0,2,1:T(8,128)(2,1)S(1)} all-to-all(bf16[256,8,576]{0,2,1:T(8,128)(2,1)S(1)} %bitcast.22), channel_id=1, replica_groups=mesh['dp'=32,'fsdp'=8] {'fsdp'}, dimensions={1} | all-to-all | bytes 4718592 | tf_op jit(solution)/shard_map/all_to_all | solution.py:36
  73.7 0.3 copy.8
  74.0 48.4 %all-gather.2.cloned.1.call-done = bf16[2048,4096]{1,0:T(8,128)(2,1)} async-done(((bf16[256,4096]{1,0:T(8,128)(2,1)}), bf16[2048,4096]{1,0:T(8,128)(2,1)}) %all-gather.2.cloned.1.call-update) | async-done | bytes 16777232 | tf_op jit(solution)/shard_map/all_gather | solution.py:38
  122.5 15.6 %convolution_bitcast_fusion = f32[4096,576]{0,1:T(8,128)} fusion(bf16[2048,576]{0,1:T(8,128)(2,1)S(1)} %bitcast.24, bf16[2048,4096]{1,0:T(8,128)(2,1)} %all-gather.2.cloned.1.call-done), kind=kOutput, calls=%fused_computation | convolution fusion | flops 9663676416 | bytes 28573696 | tf_op jit(solution)/shard_map/dot_general | solution.py:37
  138.1 0.0 reduce-scatter.2.cloned.1.call-update
  138.1 79.6 %psum.7 = s32[]{:T(128)} all-reduce(s32[]{:T(128)} %bitcast), channel_id=1, replica_groups=mesh['dp'=32,'fsdp'=8] {'dp','fsdp'}, use_global_device_ids=true, to_apply=%region_4.5 | all-reduce | flops 1 | bytes 8 | tf_op jit(solution)/shard_map/psum | solution.py:44
  218.3 148.2 %reduce-scatter.2.cloned.1.call-done = f32[128,576]{0,1:T(8,128)} async-done(((f32[4096,576]{0,1:T(8,128)}), f32[128,576]{0,1:T(8,128)}) %reduce-scatter.2.cloned.1.call-update) | async-done | bytes 294928 | tf_op jit(solution)/shard_map/reduce_scatter | solution.py:43
  366.6 0.0 copy-done.2
  366.6 1.7 add_divide_fusion
  (5 shorter events, 0.0 us)
Async XLA Ops:
  6.5 115.9 %all-gather.2.cloned.1.call-start = ((), (), s32[]{:S(2)}) async-start(), calls=%async_computation.2 | async-start | bytes 18874368 | tf_op jit(solution)/shard_map/all_gather | solution.py:38
  7.3 359.3 %reduce-scatter.2.cloned.1.call-start = ((), (), s32[]{:S(2)}) async-start(), calls=%async_computation.3 | async-start | bytes 9732096 | tf_op jit(solution)/shard_map/reduce_scatter | solution.py:43
  7.9 4.3 %copy-start.3 = (s32[1,3]{1,0:T(1,128)S(1)}, s32[1,3]{1,0:T(1,128)}, u32[]{:S(2)}) copy-start(s32[1,3]{1,0:T(1,128)} %param.8) | copy-start | bytes 40
  12.2 3.3 copy-start
  15.5 1.7 copy-start.1
  138.1 228.5 %copy-start.2 = (f32[128,576]{0,1:T(8,128)S(1)}, f32[128,576]{0,1:T(8,128)}, u32[]{:S(2)}) copy-start(f32[128,576]{0,1:T(8,128)} %param.9) | copy-start | bytes 884740
Sparse Core Ops, SparseCore 0:
  9.2 113.2 all-gather.1
  138.2 228.2 reduce-scatter.1
where the time goes:
time: 379 us; the launch traced here: 375 us
  waiting for transfers between devices  197 us (52%)
  blocking collectives  136 us (36%)
  matrix products  19.8 us (5%)
  between operations  14.8 us (4%)
  local copies, waits for them, and re-layouts  5 us (1%)
    reduce_scatter x1, waiting for transfers between devices, on_device(): lax.psum_scatter(partial_grad, 'dp', scatter_dimension=0, tiled=True)  148 us
    psum x1, blocking collectives, on_device(): admitted = lax.psum(admit_counts[0], ('dp', 'fsdp'))  79.6 us
    all_to_all x1, blocking collectives, on_device(): lax.all_to_all(clipped, 'fsdp', split_axis=1, concat_axis=0, tiled=True)  56 us
    all_gather x1, waiting for transfers between devices, on_device(): lax.all_gather(mixed_heads, 'fsdp', axis=0, tiled=True)  48.4 us
    dot_general x1, matrix products, on_device(): lax.dot_general(lax.all_gather(mixed_heads, 'fsdp', axis=0, tiled=True),...  15.6 us
  transfers between devices with their start and end apart: 2, of which 2 were waited for; matrix products, arithmetic and copies ran while one was open for 3% of the time, Pallas kernels for 0%

commit v1 on v0

v1 whole, which is shorter than its diff:
```python
import functools

import jax
import jax.numpy as jnp
from jax import lax
from jax.experimental import pallas as pl
from jax.experimental.pallas import tpu as pltpu
from jax.sharding import PartitionSpec as P

MAXSEQ = 3
CLIP = 360000
MESH = pl.DeviceIdType.MESH
NX, NY, NZ = 4, 4, 8
ROWS = 240
CUT = 112
BLOCK = 128
CHUNK = NY * BLOCK
HALF = BLOCK // 2
QUARTER = 1152
PAD = 640
F32 = jnp.float32


def quantise(value):
    top = jnp.maximum(jnp.max(jnp.abs(value), axis=0, keepdims=True), 1e-30)
    code = jnp.round(value * (32767.0 / top)).astype(jnp.int32).astype(jnp.int16)
    return code, top * (1.0 / 32767.0)


def restore(code, scale):
    return code.astype(jnp.int32).astype(F32) * scale


def kernel(
    count_ref, lengths_ref, x_hbm, g_hbm, noise_ref, out_ref,
    xs, graw, gcut, gs, acc, away, near, total, ysend, yscale, yrecv, yrscale,
    zsend, zscale, zrecv, zrscale, fin_send, fin_recv, tally,
    load_sem, g_sem, xsend_sem, xrecv_sem, gsend_sem, grecv_sem, dsend_sem, drecv_sem,
    ysend_sem, yrecv_sem, ysend2_sem, yrecv2_sem, zsend_sem, zrecv_sem, zsend2_sem, zrecv2_sem,
    fsend_sem, frecv_sem, csend_sem, crecv_sem,
):
    dp = lax.axis_index("dp")
    fs = lax.axis_index("fsdp")
    x, core = fs // 2, fs % 2
    y, z = dp // NZ, dp % NZ

    def device(dx=0, dy=0, dz=0, dc=0):
        return (
            lax.rem(y + dy, NY) * NZ + lax.rem(z + dz, NZ),
            lax.rem(x + dx, NX) * 2 + lax.rem(core + dc, 2),
        )

    partners = (
        [device(dx=d) for d in (1, 2, 3)]
        + [device(dy=d) for d in (1, 2, 3)]
        + [device(dz=d) for d in range(1, NZ)]
        + [device(dc=1)]
    )
    barrier = pltpu.get_barrier_semaphore()
    for partner in partners:
        pl.semaphore_signal(barrier, inc=1, device_id=partner, device_id_type=MESH)

    def target(t):
        return lax.rem(z + 1 + t, NZ)

    def load(t, j):
        at = pl.multiple_of((j * NZ + target(t)) * BLOCK, BLOCK)
        return pltpu.make_async_copy(
            x_hbm.at[pl.ds(0, ROWS), pl.ds(at, BLOCK)],
            xs.at[t, pl.ds(0, ROWS), pl.ds(j * BLOCK, BLOCK)],
            load_sem.at[t, j],
        )

    def remote(src, dst, send, recv, to):
        return pltpu.make_async_remote_copy(
            src_ref=src, dst_ref=dst, send_sem=send, recv_sem=recv, device_id=to, device_id_type=MESH
        )

    def x_copy(t, k):
        if k == 0:
            src, dst, to = pl.ds(0, ROWS), pl.ds(ROWS, ROWS), device(dx=1)
        elif k == 1:
            src, dst, to = pl.ds(0, ROWS), pl.ds(2 * ROWS, ROWS), device(dx=3)
        elif k == 2:
            src, dst, to = pl.ds(ROWS, CUT), pl.ds(3 * ROWS, CUT), device(dx=1)
        else:
            src, dst, to = pl.ds(2 * ROWS + CUT, ROWS - CUT), pl.ds(3 * ROWS + CUT, ROWS - CUT), device(dx=3)
        return remote(xs.at[t, src], xs.at[t, dst], xsend_sem.at[t, k], xrecv_sem.at[t, k], to)

    def g_copy(k):
        d = (1, 3, 2)[k]
        return remote(
            gcut.at[lax.rem(x + d, NX)], gs.at[pl.ds((k + 1) * ROWS, ROWS)], gsend_sem.at[k], grecv_sem.at[k], device(dx=d)
        )

    def d_copy(t):
        return remote(away.at[t], near.at[t], dsend_sem.at[t], drecv_sem.at[t], device(dc=1))

    def y_copy(t, k):
        to = device(dy=k + 1)
        return (
            remote(ysend.at[t, k], yrecv.at[t, k], ysend_sem.at[t, k], yrecv_sem.at[t, k], to),
            remote(yscale.at[t, k], yrscale.at[t, k], ysend2_sem.at[t, k], yrecv2_sem.at[t, k], to),
        )

    def z_copy(t):
        to = device(dz=t + 1)
        return (
            remote(zsend.at[t], zrecv.at[t], zsend_sem.at[t], zrecv_sem.at[t], to),
            remote(zscale.at[t], zrscale.at[t], zsend2_sem.at[t], zrecv2_sem.at[t], to),
        )

    stages = (("dc", (1,)), ("dx", (1, 2, 3)), ("dy", (1, 2, 3)), ("dz", tuple(range(1, NZ))))
    first = (0, 1, 4, 7, 14)

    def c_copy(stage, i):
        axis, steps = stages[stage]
        slot = first[stage] + i
        return remote(
            tally.at[0, stage], tally.at[1, slot], csend_sem.at[slot], crecv_sem.at[slot], device(**{axis: steps[i]})
        )

    def count_send(stage):
        for i in range(len(stages[stage][1])):
            c_copy(stage, i).start()

    def count_take(stage):
        value = tally[0, stage]
        for i in range(len(stages[stage][1])):
            c_copy(stage, i).wait()
            value = value + tally[1, first[stage] + i]
        return value

    for t in range(NZ):
        for j in range(NY):
            load(t, j).start()
    g_load = pltpu.make_async_copy(g_hbm.at[pl.ds(0, ROWS)], graw, g_sem)
    g_load.start()
    tally[0, 0] = jnp.full((8, 128), count_ref[0], jnp.int32)

    pl.semaphore_wait(barrier, len(partners))

    for t in range(2):
        for j in range(NY):
            load(t, j).wait()
        x_copy(t, 0).start()
        x_copy(t, 1).start()
    count_send(0)

    for t in range(2, NZ):
        for j in range(NY):
            load(t, j).wait()
    own = xs[0, pl.ds(0, ROWS)]
    act = lax.dot_general(own, own, (((1,), (1,)), ((), ())), preferred_element_type=F32)
    for t in range(1, NZ):
        own = xs[t, pl.ds(0, ROWS)]
        act += lax.dot_general(own, own, (((1,), (1,)), ((), ())), preferred_element_type=F32)
    g_load.wait()
    grad = jnp.zeros((ROWS, ROWS), F32)
    for q in range(NX):
        part = graw[:, pl.ds(q * QUARTER, QUARTER)]
        grad += lax.dot_general(part, part, (((1,), (1,)), ((), ())), preferred_element_type=F32)
    product = act * grad
    row = lax.broadcasted_iota(jnp.int32, (ROWS, ROWS), 0)
    col = lax.broadcasted_iota(jnp.int32, (ROWS, ROWS), 1)
    line = lax.broadcasted_iota(jnp.int32, (ROWS, 1), 0)
    scale = jnp.zeros((ROWS, 1), F32)
    start = jnp.int32(0)
    for j in range(MAXSEQ):
        used = jnp.where(j < count_ref[0], lengths_ref[0, j], 0)
        end = start + used
        both = (row >= start) & (row < end) & (col >= start) & (col < end)
        sums = jnp.sum(jnp.where(both, product, 0.0), axis=1, keepdims=True)
        norm_sq = jnp.sum(sums, axis=0, keepdims=True)
        factor = CLIP / jnp.maximum(jnp.sqrt(norm_sq), F32(CLIP))
        scale = jnp.where((line >= start) & (line < end), factor, scale)
        start = end
    for q in range(NX):
        gcut[q] = (scale * graw[:, pl.ds(q * QUARTER, QUARTER)].astype(F32)).astype(jnp.bfloat16)
    for k in range(3):
        g_copy(k).start()
    gs[pl.ds(0, ROWS)] = gcut[x]

    def step(i, carry):
        @pl.when(i + 2 < NZ)
        def _():
            x_copy(i + 2, 0).start()
            x_copy(i + 2, 1).start()

        @pl.when(i < NZ)
        def _():
            x_copy(i, 0).wait_recv()
            x_copy(i, 1).wait_recv()
            x_copy(i, 2).start()
            x_copy(i, 3).start()

        @pl.when(i == 0)
        def _():
            for k in range(3):
                g_copy(k).wait()

        @pl.when((i >= 1) & (i < NZ + 1))
        def _():
            t = i - 1
            x_copy(t, 2).wait_recv()
            x_copy(t, 3).wait_recv()
            for pair in range(NY // 2):
                tile = lax.dot_general(
                    xs[t, :, pl.ds(pair * 2 * BLOCK, 2 * BLOCK)], gs[...], (((0,), (0,)), ((), ())),
                    preferred_element_type=F32,
                )
                for k in range(2):
                    for h in range(2):
                        acc[h, 2 * pair + k] = tile[k * BLOCK + h * HALF : k * BLOCK + (h + 1) * HALF]
            away[t] = acc[1 - core]
            total[t] = acc[core]
            d_copy(t).start()

        for stage in range(4):
            @pl.when(i == 2 * stage + 1)
            def _(stage=stage):
                value = count_take(stage)
                tally[0, stage + 1] = value
                if stage < 3:
                    count_send(stage + 1)

        @pl.when((i >= 2) & (i < NZ + 2))
        def _():
            t = i - 2
            d_copy(t).wait_recv()
            for k in range(3):
                to = lax.rem(y + k + 1, NY)
                code, factor = quantise(total[t, to] + near[t, to])
                ysend[t, k] = code
                yscale[t, k] = factor
                for copy in y_copy(t, k):
                    copy.start()

        @pl.when((i >= 3) & (i < NZ + 3))
        def _():
            t = i - 3
            value = total[t, y] + near[t, y]
            for k in range(3):
                for copy in y_copy(t, k):
                    copy.wait_recv()
                value += restore(yrecv[t, k], yrscale[t, k])

            @pl.when(t < NZ - 1)
            def _():
                code, factor = quantise(value)
                zsend[t] = code
                zscale[t] = factor
                for copy in z_copy(t):
                    copy.start()

            @pl.when(t == NZ - 1)
            def _():
                fin_send[...] = value

        return carry

    lax.fori_loop(0, NZ + 3, step, 0)

    value = fin_send[...]
    for t in range(NZ - 1):
        for copy in z_copy(t):
            copy.wait_recv()
        value += restore(zrecv[t], zrscale[t])
    fin_send[...] = value
    other = pl.multiple_of((1 - core) * (QUARTER - PAD), 128)
    last = remote(fin_send.at[:, pl.ds(other, PAD)], fin_recv, fsend_sem, frecv_sem, device(dc=1))
    last.start()
    admitted = tally[0, 4, 0:1, 0:1].astype(F32)

    def finish(c, part, rows):
        lo = c * (PAD - 576)
        out_ref[rows] = (part[:, lo : lo + 576] + noise_ref[rows]) / admitted

    for c in range(2):
        @pl.when(core == c)
        def _(c=c):
            mine = fin_send[:, c * (QUARTER - PAD) : c * (QUARTER - PAD) + PAD]
            finish(c, mine, slice(c * HALF, (c + 1) * HALF))

    last.wait()
    for c in range(2):
        @pl.when(core == c)
        def _(c=c):
            finish(c, fin_recv[...], slice((1 - c) * HALF, (2 - c) * HALF))

    def drain(t, carry):
        for k in range(4):
            x_copy(t, k).wait_send()
        d_copy(t).wait_send()
        for k in range(3):
            for copy in y_copy(t, k):
                copy.wait_send()
        return carry

    lax.fori_loop(0, NZ, drain, 0)
    for t in range(NZ - 1):
        for copy in z_copy(t):
            copy.wait_send()


def on_device(mixed_heads, out_grads, admit_counts, lengths, gauss_noise):
    dma = pltpu.SemaphoreType.DMA
    bf16, i16 = jnp.bfloat16, jnp.int16
    inner, width = mixed_heads.shape[1], out_grads.shape[1]
    return pl.pallas_call(
        kernel,
        out_shape=jax.ShapeDtypeStruct(gauss_noise.shape, F32),
        in_specs=[
            pl.BlockSpec(memory_space=pltpu.SMEM),
            pl.BlockSpec(memory_space=pltpu.SMEM),
            pl.BlockSpec(memory_space=pl.ANY),
            pl.BlockSpec(memory_space=pl.ANY),
            pl.BlockSpec(memory_space=pltpu.VMEM),
        ],
        out_specs=pl.BlockSpec(memory_space=pltpu.VMEM),
        scratch_shapes=[
            pltpu.VMEM((NZ, NX * ROWS, CHUNK), bf16),
            pltpu.VMEM((ROWS, width), bf16),
            pltpu.VMEM((NX, ROWS, QUARTER), bf16),
            pltpu.VMEM((NX * ROWS, QUARTER), bf16),
            pltpu.VMEM((2, NY, HALF, QUARTER), F32),
            pltpu.VMEM((NZ, NY, HALF, QUARTER), F32),
            pltpu.VMEM((NZ, NY, HALF, QUARTER), F32),
            pltpu.VMEM((NZ, NY, HALF, QUARTER), F32),
            pltpu.VMEM((NZ, 3, HALF, QUARTER), i16),
            pltpu.VMEM((NZ, 3, 1, QUARTER), F32),
            pltpu.VMEM((NZ, 3, HALF, QUARTER), i16),
            pltpu.VMEM((NZ, 3, 1, QUARTER), F32),
            pltpu.VMEM((NZ - 1, HALF, QUARTER), i16),
            pltpu.VMEM((NZ - 1, 1, QUARTER), F32),
            pltpu.VMEM((NZ - 1, HALF, QUARTER), i16),
            pltpu.VMEM((NZ - 1, 1, QUARTER), F32),
            pltpu.VMEM((HALF, QUARTER), F32),
            pltpu.VMEM((HALF, PAD), F32),
            pltpu.VMEM((2, 14, 8, 128), jnp.int32),
            dma((NZ, NY)),
            dma,
            dma((NZ, 4)),
            dma((NZ, 4)),
            dma((3,)),
            dma((3,)),
            dma((NZ,)),
            dma((NZ,)),
            dma((NZ, 3)),
            dma((NZ, 3)),
            dma((NZ, 3)),
            dma((NZ, 3)),
            dma((NZ - 1,)),
            dma((NZ - 1,)),
            dma((NZ - 1,)),
            dma((NZ - 1,)),
            dma,
            dma,
            dma((14,)),
            dma((14,)),
        ],
        compiler_params=pltpu.CompilerParams(
            collective_id=0, has_side_effects=True, vmem_limit_bytes=63 * 1024 * 1024
        ),
        cost_estimate=pl.CostEstimate(flops=10**10, bytes_accessed=5 * 10**6, transcendentals=0),
    )(admit_counts, lengths, mixed_heads, out_grads, gauss_noise)


def solution(mesh):
    in_specs = (
        P(("dp", "fsdp"), None),
        P(("dp", "fsdp"), None),
        P(("dp", "fsdp")),
        P(("dp", "fsdp"), None),
        P("dp", "fsdp"),
    )
    return jax.shard_map(
        on_device, mesh=mesh, in_specs=in_specs, out_specs=P("dp", "fsdp"), check_vma=False
    )
```

time: 379 us -> 135 us (0.36); the launches traced: 375 us -> 135 us
  waiting for transfers between devices: 197 us -> 0 us
  blocking collectives: 136 us -> 0 us
  Pallas kernels: 0 us -> 131 us
  matrix products: 19.8 us -> 0 us
  between operations: 14.8 us -> 0.66 us
    reduce_scatter x1 -> x0, waiting for transfers between devices: 148 us -> none  [on_device(): lax.psum_scatter(partial_grad, 'dp', scatter_dimension=0, tiled=True)]
    pallas_call x0 -> x1, Pallas kernels: none -> 131 us  [on_device(): pl.pallas_call(kernel, out_shape=jax.ShapeDtypeStruct(gauss_noise.shape,...]
    psum x1 -> x0, blocking collectives: 79.6 us -> none  [on_device(): admitted = lax.psum(admit_counts[0], ('dp', 'fsdp'))]
    all_to_all x1 -> x0, blocking collectives: 56 us -> none  [on_device(): lax.all_to_all(clipped, 'fsdp', split_axis=1, concat_axis=0, tiled=True)]
    all_gather x1 -> x0, waiting for transfers between devices: 48.4 us -> none  [on_device(): lax.all_gather(mixed_heads, 'fsdp', axis=0, tiled=True)]
    dot_general x4 -> x0, matrix products: 19.8 us -> none  [the longest x1 15.6 us: on_device(): lax.dot_general(lax.all_gather(mixed_heads, 'fsdp', axis=0, tiled=True),...]
  transfers between devices with their start and end apart: 2 -> 0, of which waited for: 2 -> 0; matrix products, arithmetic and copies ran while one was open for 3% -> 0% of each run, Pallas kernels for 0% -> 0%
where the time goes in v1:
time: 135 us
  Pallas kernels  131 us (97%)
  local copies, waits for them, and re-layouts  3.68 us (3%)
    pallas_call x1, Pallas kernels, on_device(): pl.pallas_call(kernel, out_shape=jax.ShapeDtypeStruct(gauss_noise.shape,...  131 us

profile of v1, /device:TPU:1, one launch (start us, length us, event | category | flops | bytes accessed | tf_op | source)
XLA Modules:
  0.0 135.0 jit_solution(1278231054934216405)
XLA Ops:
  0.7 1.8 %copy.6.noise_ref = f32[128,576]{1,0:T(8,128)} copy(f32[128,576]{0,1:T(8,128)} %param.9) | data formatting | bytes 589824 | tf_op args[4]
  2.5 130.6 %shard_map.55 = f32[128,576]{1,0:T(8,128)} custom-call(s32[1]{0:T(128)S(6)} %copy.8.count_ref, s32[1,3]{1,0:T(1,128)} %lengths_ref.1, bf16[256,4096]{1,0:T(8,128)(2,1)} %x_hbm.1, bf16[256,4608]{1,0:T(8,128)(2,1)} %g_hbm.1, f32[128,576]{1,0:T(8,128)} %copy.6.noise_ref), custom_call_target="tpu_custom_call" | custom-call | flops 10000000000 | bytes 5000000 | tf_op jit(solution)/shard_map/pallas_call | solution.py:310
  133.1 1.8 %copy.7 = f32[128,576]{0,1:T(8,128)} copy(f32[128,576]{1,0:T(8,128)} %shard_map.55) | data formatting | bytes 589824 | tf_op jit(solution)/shard_map/pallas_call | solution.py:310

commit v2 on v1

v2 whole, which is shorter than its diff:
```python
import functools

import jax
import jax.numpy as jnp
from jax import lax
from jax.experimental import pallas as pl
from jax.experimental.pallas import tpu as pltpu
from jax.sharding import PartitionSpec as P

MAXSEQ = 3
CLIP = 360000
MESH = pl.DeviceIdType.MESH
NX, NY, NZ = 4, 4, 8
ROWS = 240
FEW = 160
MOVED = 32
KEPT = ROWS - MOVED
CUT = 112
BLOCK = 128
CHUNK = NY * BLOCK
HALF = BLOCK // 2
SIDE = HALF // 2
QUARTER = 1152
WIDTH = 576
PAD = 640
F32 = jnp.float32


def quantise(value):
    top = jnp.maximum(jnp.max(jnp.abs(value), axis=0, keepdims=True), 1e-30)
    code = jnp.round(value * (32767.0 / top)).astype(jnp.int32).astype(jnp.int16)
    return code, top * (1.0 / 32767.0)


def restore(code, scale):
    return code.astype(jnp.int32).astype(F32) * scale


def kernel(
    count_ref, lengths_ref, x_hbm, g_hbm, noise_ref, out_ref,
    xraw, xmove, xs, graw, gcut, gs, part, near,
    asend, ascale, arecv, arscale, ysend, yscale, yrecv, yrscale,
    zsend, zscale, zrecv, zrscale, fin_send, full, turned, tally,
    load_sem, msend_sem, mrecv_sem, xsend_sem, xrecv_sem, gsend_sem, grecv_sem, dsend_sem, drecv_sem,
    asend_sem, arecv_sem, ysend_sem, yrecv_sem, zsend_sem, zrecv_sem,
    fsend_sem, frecv_sem, csend_sem, crecv_sem,
):
    dp = lax.axis_index("dp")
    fs = lax.axis_index("fsdp")
    x, core = fs // 2, fs % 2
    y, z = dp // NZ, dp % NZ

    def device(dx=0, dy=0, dz=0, dc=0):
        return (
            lax.rem(y + dy, NY) * NZ + lax.rem(z + dz, NZ),
            lax.rem(x + dx, NX) * 2 + lax.rem(core + dc, 2),
        )

    partners = (
        [device(dx=d) for d in (1, 2, 3)]
        + [device(dy=d) for d in (1, 2, 3)]
        + [device(dz=d) for d in range(1, NZ)]
        + [device(dc=1)]
    )
    barrier = pltpu.get_barrier_semaphore()
    for partner in partners:
        pl.semaphore_signal(barrier, inc=1, device_id=partner, device_id_type=MESH)

    x_load = pltpu.make_async_copy(x_hbm.at[pl.ds(0, ROWS)], xraw, load_sem.at[0])
    g_load = pltpu.make_async_copy(g_hbm.at[pl.ds(0, ROWS)], graw, load_sem.at[1])
    x_load.start()
    g_load.start()
    tally[0, 0] = jnp.full((8, 128), count_ref[0], jnp.int32)

    def target(t):
        return lax.rem(z + 1 + t, NZ)

    def remote(src, dst, send, recv, to):
        return pltpu.make_async_remote_copy(
            src_ref=src, dst_ref=dst, send_sem=send, recv_sem=recv, device_id=to, device_id_type=MESH
        )

    mate = device(dy=lax.rem(7 - 2 * y, NY))

    def move(k):
        if k == 2:
            src, dst = gcut.at[:, pl.ds(KEPT, MOVED)], gcut.at[:, pl.ds(FEW, MOVED)]
        else:
            steps = pl.ds(0, 2) if k == 0 else pl.ds(2, NZ - 2)
            src, dst = xmove.at[steps], xs.at[steps, pl.ds(FEW, MOVED)]
        return remote(src, dst, msend_sem.at[k], mrecv_sem.at[k], mate)

    def x_copy(t, k):
        if k == 0:
            src, dst, to = pl.ds(0, KEPT), pl.ds(KEPT, KEPT), device(dx=1)
        elif k == 1:
            src, dst, to = pl.ds(0, KEPT), pl.ds(2 * KEPT, KEPT), device(dx=3)
        elif k == 2:
            src, dst, to = pl.ds(KEPT, CUT), pl.ds(3 * KEPT, CUT), device(dx=1)
        else:
            src, dst, to = pl.ds(2 * KEPT + CUT, KEPT - CUT), pl.ds(3 * KEPT + CUT, KEPT - CUT), device(dx=3)
        return remote(xs.at[t, src], xs.at[t, dst], xsend_sem.at[t, k], xrecv_sem.at[t, k], to)

    def g_copy(k):
        d = (1, 3, 2)[k]
        return remote(
            gcut.at[lax.rem(x + d, NX), pl.ds(0, KEPT)], gs.at[pl.ds((k + 1) * KEPT, KEPT)],
            gsend_sem.at[k], grecv_sem.at[k], device(dx=d),
        )

    def d_copy(t):
        return remote(part.at[1 - core, t], near.at[t], dsend_sem.at[t], drecv_sem.at[t], device(dc=1))

    def a_copy(t, k):
        to = device(dy=(1, 3)[k])
        return (
            remote(asend.at[t, k], arecv.at[t, k], asend_sem.at[t, k, 0], arecv_sem.at[t, k, 0], to),
            remote(ascale.at[t, k], arscale.at[t, k], asend_sem.at[t, k, 1], arecv_sem.at[t, k, 1], to),
        )

    def y_copy(t, k):
        to = device(dy=(1, 3)[k])
        return (
            remote(ysend.at[t, k], yrecv.at[t, k], ysend_sem.at[t, k, 0], yrecv_sem.at[t, k, 0], to),
            remote(yscale.at[t, k], yrscale.at[t, k], ysend_sem.at[t, k, 1], yrecv_sem.at[t, k, 1], to),
        )

    def z_copy(t):
        to = device(dz=t + 1)
        return (
            remote(zsend.at[t], zrecv.at[t], zsend_sem.at[t, 0], zrecv_sem.at[t, 0], to),
            remote(zscale.at[t], zrscale.at[t], zsend_sem.at[t, 1], zrecv_sem.at[t, 1], to),
        )

    stages = (("dc", (1,)), ("dx", (1, 2, 3)), ("dy", (1, 2, 3)), ("dz", tuple(range(1, NZ))))
    first = (0, 1, 4, 7, 14)

    def c_copy(stage, i):
        axis, steps = stages[stage]
        slot = first[stage] + i
        return remote(
            tally.at[0, stage], tally.at[1, slot], csend_sem.at[slot], crecv_sem.at[slot], device(**{axis: steps[i]})
        )

    def count_send(stage):
        for i in range(len(stages[stage][1])):
            c_copy(stage, i).start()

    def count_take(stage):
        value = tally[0, stage]
        for i in range(len(stages[stage][1])):
            c_copy(stage, i).wait()
            value = value + tally[1, first[stage] + i]
        return value

    many = y >= NY // 2
    x_load.wait()

    def gather(t, carry):
        for j in range(NY):
            at = pl.multiple_of((j * NZ + target(t)) * BLOCK, BLOCK)
            to = slice(j * BLOCK, (j + 1) * BLOCK)
            xs[t, 0:FEW, to] = xraw[0:FEW, pl.ds(at, BLOCK)]
            xs[t, FEW + MOVED : KEPT, to] = xraw[FEW + MOVED : KEPT, pl.ds(at, BLOCK)]
            xmove[t, :, to] = xraw[KEPT:ROWS, pl.ds(at, BLOCK)]

            @pl.when(many)
            def _():
                xs[t, FEW : FEW + MOVED, to] = xraw[FEW : FEW + MOVED, pl.ds(at, BLOCK)]

        return carry

    lax.fori_loop(0, NZ, gather, 0)
    pl.semaphore_wait(barrier, len(partners))

    @pl.when(many)
    def _():
        move(0).start()
        move(1).start()

    count_send(0)

    @pl.when(jnp.logical_not(many))
    def _():
        move(0).wait_recv()

    for t in range(2):
        x_copy(t, 0).start()
        x_copy(t, 1).start()

    own = xraw[...]
    act = lax.dot_general(own, own, (((1,), (1,)), ((), ())), preferred_element_type=F32)
    g_load.wait()
    own = graw[...]
    grad = lax.dot_general(own, own, (((1,), (1,)), ((), ())), preferred_element_type=F32)
    product = act * grad
    row = lax.broadcasted_iota(jnp.int32, (ROWS, ROWS), 0)
    col = lax.broadcasted_iota(jnp.int32, (ROWS, ROWS), 1)
    line = lax.broadcasted_iota(jnp.int32, (ROWS, 1), 0)
    scale = jnp.zeros((ROWS, 1), F32)
    start = jnp.int32(0)
    for j in range(MAXSEQ):
        used = jnp.where(j < count_ref[0], lengths_ref[0, j], 0)
        end = start + used
        both = (row >= start) & (row < end) & (col >= start) & (col < end)
        sums = jnp.sum(jnp.where(both, product, 0.0), axis=1, keepdims=True)
        norm_sq = jnp.sum(sums, axis=0, keepdims=True)
        factor = CLIP / jnp.maximum(jnp.sqrt(norm_sq), F32(CLIP))
        scale = jnp.where((line >= start) & (line < end), factor, scale)
        start = end

    def clip(q, lo, hi):
        rows = graw[lo:hi, q * QUARTER : (q + 1) * QUARTER].astype(F32)
        gcut[q, lo:hi] = (scale[lo:hi] * rows).astype(jnp.bfloat16)

    for q in range(NX):
        clip(q, FEW + MOVED, ROWS)

    @pl.when(many)
    def _():
        move(2).start()
        for q in range(NX):
            clip(q, FEW, FEW + MOVED)

    for q in range(NX):
        clip(q, 0, FEW)

    for t in range(2):
        x_copy(t, 0).wait_recv()
        x_copy(t, 1).wait_recv()
        x_copy(t, 2).start()
        x_copy(t, 3).start()

    @pl.when(jnp.logical_not(many))
    def _():
        move(2).wait_recv()
        move(1).wait_recv()

    for k in range(3):
        g_copy(k).start()
    x_copy(2, 0).start()
    x_copy(2, 1).start()
    gs[0:KEPT] = gcut[x, 0:KEPT]

    def step(i, carry):
        @pl.when(i + 2 < NZ)
        def _():
            x_copy(i + 2, 0).start()
            x_copy(i + 2, 1).start()

        @pl.when((i >= 2) & (i < NZ))
        def _():
            x_copy(i, 0).wait_recv()
            x_copy(i, 1).wait_recv()
            x_copy(i, 2).start()
            x_copy(i, 3).start()

        @pl.when(i == 1)
        def _():
            for k in range(3):
                g_copy(k).wait()

        @pl.when(i < NZ + 1)
        def _():
            t = i - 1
            x_copy(t, 2).wait_recv()
            x_copy(t, 3).wait_recv()
            for pair in range(NY // 2):
                tile = lax.dot_general(
                    xs[t, :, pair * 2 * BLOCK : (pair + 1) * 2 * BLOCK], gs[...], (((0,), (0,)), ((), ())),
                    preferred_element_type=F32,
                )
                for k in range(2):
                    for h in range(2):
                        part[h, t, 2 * pair + k] = tile[k * BLOCK + h * HALF : k * BLOCK + (h + 1) * HALF]
            d_copy(t).start()

        for stage in range(4):
            @pl.when(i == 2 * stage + 1)
            def _(stage=stage):
                value = count_take(stage)
                tally[0, stage + 1] = value
                if stage < 3:
                    count_send(stage + 1)

        ahead, behind = lax.rem(y + 1, NY), lax.rem(y + 3, NY)
        far = lax.rem(y + 2, NY)

        @pl.when((i >= 2) & (i < NZ + 2))
        def _():
            t = i - 2
            d_copy(t).wait_recv()
            for k in range(2):
                rows = slice(k * SIDE, (k + 1) * SIDE)
                code, factor = quantise(part[core, t, far, rows] + near[t, far, rows])
                asend[t, k] = code
                ascale[t, k] = factor
                for copy in a_copy(t, k):
                    copy.start()

        @pl.when((i >= 3) & (i < NZ + 3))
        def _():
            t = i - 3
            for k in range(2):
                to = (ahead, behind)[k]
                value = part[core, t, to] + near[t, to]
                for copy in a_copy(t, k):
                    copy.wait_recv()
                more = restore(arecv[t, k], arscale[t, k])
                if k == 0:
                    value = jnp.concatenate([value[:SIDE] + more, value[SIDE:]], axis=0)
                else:
                    value = jnp.concatenate([value[:SIDE], value[SIDE:] + more], axis=0)
                code, factor = quantise(value)
                ysend[t, k] = code
                yscale[t, k] = factor
                for copy in y_copy(t, k):
                    copy.start()

        @pl.when(i >= 4)
        def _():
            t = i - 4
            value = part[core, t, y] + near[t, y]
            for k in range(2):
                for copy in y_copy(t, k):
                    copy.wait_recv()
                value += restore(yrecv[t, k], yrscale[t, k])

            @pl.when(t < NZ - 1)
            def _():
                code, factor = quantise(value)
                zsend[t] = code
                zscale[t] = factor
                for copy in z_copy(t):
                    copy.start()

            @pl.when(t == NZ - 1)
            def _():
                fin_send[...] = value

        return carry

    lax.fori_loop(1, NZ + 4, step, 0)

    value = fin_send[...]
    for t in range(NZ - 1):
        for copy in z_copy(t):
            copy.wait_recv()
        value += restore(zrecv[t], zrscale[t])
    fin_send[...] = value
    shift = QUARTER - PAD
    mine = pl.ds(pl.multiple_of(core * HALF, HALF), HALF)
    last = remote(
        fin_send.at[:, pl.ds(pl.multiple_of((1 - core) * shift, BLOCK), PAD)], full.at[mine], fsend_sem, frecv_sem,
        device(dc=1),
    )
    last.start()
    full[mine] = fin_send[:, pl.ds(pl.multiple_of(core * shift, BLOCK), PAD)]
    admitted = tally[0, 4, 0:1, 0:1].astype(F32)

    def drain(t, carry):
        for k in range(4):
            x_copy(t, k).wait_send()
        d_copy(t).wait_send()
        for k in range(2):
            for copy in a_copy(t, k) + y_copy(t, k):
                copy.wait_send()
        return carry

    lax.fori_loop(0, NZ, drain, 0)
    for t in range(NZ - 1):
        for copy in z_copy(t):
            copy.wait_send()

    @pl.when(many)
    def _():
        for k in range(3):
            move(k).wait_send()

    last.wait()
    turned[...] = jnp.transpose(full[...])
    lead = pl.multiple_of(core * (PAD - WIDTH), PAD - WIDTH)
    out_ref[...] = (turned[pl.ds(lead, WIDTH)] + noise_ref[...]) / admitted


def on_device(mixed_heads, out_grads, admit_counts, lengths, gauss_noise):
    dma = pltpu.SemaphoreType.DMA
    bf16, i16 = jnp.bfloat16, jnp.int16
    inner, width = mixed_heads.shape[1], out_grads.shape[1]
    turned = pl.pallas_call(
        kernel,
        out_shape=jax.ShapeDtypeStruct(gauss_noise.shape[::-1], F32),
        in_specs=[
            pl.BlockSpec(memory_space=pltpu.SMEM),
            pl.BlockSpec(memory_space=pltpu.SMEM),
            pl.BlockSpec(memory_space=pl.ANY),
            pl.BlockSpec(memory_space=pl.ANY),
            pl.BlockSpec(memory_space=pltpu.VMEM),
        ],
        out_specs=pl.BlockSpec(memory_space=pltpu.VMEM),
        scratch_shapes=[
            pltpu.VMEM((ROWS, inner), bf16),
            pltpu.VMEM((NZ, MOVED, CHUNK), bf16),
            pltpu.VMEM((NZ, NX * KEPT, CHUNK), bf16),
            pltpu.VMEM((ROWS, width), bf16),
            pltpu.VMEM((NX, ROWS, QUARTER), bf16),
            pltpu.VMEM((NX * KEPT, QUARTER), bf16),
            pltpu.VMEM((2, NZ, NY, HALF, QUARTER), F32),
            pltpu.VMEM((NZ, NY, HALF, QUARTER), F32),
            pltpu.VMEM((NZ, 2, SIDE, QUARTER), i16),
            pltpu.VMEM((NZ, 2, 1, QUARTER), F32),
            pltpu.VMEM((NZ, 2, SIDE, QUARTER), i16),
            pltpu.VMEM((NZ, 2, 1, QUARTER), F32),
            pltpu.VMEM((NZ, 2, HALF, QUARTER), i16),
            pltpu.VMEM((NZ, 2, 1, QUARTER), F32),
            pltpu.VMEM((NZ, 2, HALF, QUARTER), i16),
            pltpu.VMEM((NZ, 2, 1, QUARTER), F32),
            pltpu.VMEM((NZ - 1, HALF, QUARTER), i16),
            pltpu.VMEM((NZ - 1, 1, QUARTER), F32),
            pltpu.VMEM((NZ - 1, HALF, QUARTER), i16),
            pltpu.VMEM((NZ - 1, 1, QUARTER), F32),
            pltpu.VMEM((HALF, QUARTER), F32),
            pltpu.VMEM((BLOCK, PAD), F32),
            pltpu.VMEM((PAD, BLOCK), F32),
            pltpu.VMEM((2, 14, 8, 128), jnp.int32),
            dma((2,)),
            dma((3,)),
            dma((3,)),
            dma((NZ, 4)),
            dma((NZ, 4)),
            dma((3,)),
            dma((3,)),
            dma((NZ,)),
            dma((NZ,)),
            dma((NZ, 2, 2)),
            dma((NZ, 2, 2)),
            dma((NZ, 2, 2)),
            dma((NZ, 2, 2)),
            dma((NZ - 1, 2)),
            dma((NZ - 1, 2)),
            dma,
            dma,
            dma((14,)),
            dma((14,)),
        ],
        compiler_params=pltpu.CompilerParams(
            collective_id=0, has_side_effects=True, vmem_limit_bytes=63 * 1024 * 1024
        ),
        cost_estimate=pl.CostEstimate(flops=10**10, bytes_accessed=5 * 10**6, transcendentals=0),
    )(admit_counts, lengths, mixed_heads, out_grads, gauss_noise.T)
    return turned.T


def solution(mesh):
    in_specs = (
        P(("dp", "fsdp"), None),
        P(("dp", "fsdp"), None),
        P(("dp", "fsdp")),
        P(("dp", "fsdp"), None),
        P("dp", "fsdp"),
    )
    return jax.shard_map(
        on_device, mesh=mesh, in_specs=in_specs, out_specs=P("dp", "fsdp"), check_vma=False
    )
```

time: 135 us -> 130 us (0.963)
  Pallas kernels: 131 us -> 128 us
  local copies, waits for them, and re-layouts: 3.68 us -> 1.69 us
    pallas_call x1, Pallas kernels: 131 us -> 128 us  [on_device(): pl.pallas_call(kernel, out_shape=jax.ShapeDtypeStruct(gauss_noise.shape[:...]
    pallas_call x1 -> x0, local copies, waits for them, and re-layouts: 1.84 us -> none  [on_device(): pl.pallas_call(kernel, out_shape=jax.ShapeDtypeStruct(gauss_noise.shape,...]
where the time goes in v2:
time: 130 us
  Pallas kernels  128 us (98%)
  local copies, waits for them, and re-layouts  1.69 us (1%)
    pallas_call x1, Pallas kernels, on_device(): pl.pallas_call(kernel, out_shape=jax.ShapeDtypeStruct(gauss_noise.shape[:...  128 us

profile of v2, /device:TPU:1, one launch (start us, length us, event | category | flops | bytes accessed | tf_op | source)
XLA Modules:
  0.0 130.3 jit_solution(4382709400638562960)
XLA Ops:
  0.7 127.9 %shard_map.55 = f32[576,128]{1,0:T(8,128)} custom-call(s32[1]{0:T(128)S(6)} %copy.7.count_ref, s32[1,3]{1,0:T(1,128)} %lengths_ref.1, bf16[256,4096]{1,0:T(8,128)(2,1)} %x_hbm.1, bf16[256,4608]{1,0:T(8,128)(2,1)} %g_hbm.1, f32[576,128]{1,0:T(8,128)} %bitcast.3), custom_call_target="tpu_custom_call" | custom-call | flops 10000000000 | bytes 5000000 | tf_op jit(solution)/shard_map/pallas_call | solution.py:390
  128.6 1.7 %copy.8 = f32[128,576]{0,1:T(8,128)} copy(f32[128,576]{0,1:T(8,128)} %bitcast.2) | data formatting | bytes 589824

commit v3 on v2

--- a/solution.py
+++ b/solution.py
@@ -21,6 +21,10 @@
 HALF = BLOCK // 2
 SIDE = HALF // 2
 QUARTER = 1152
+PARTS = 3
+COLS = QUARTER // PARTS
+UNITS = NZ * PARTS
+SENT = UNITS - PARTS
 WIDTH = 576
 PAD = 640
 F32 = jnp.float32
@@ -90,6 +94,15 @@
             src, dst = xmove.at[steps], xs.at[steps, pl.ds(FEW, MOVED)]
         return remote(src, dst, msend_sem.at[k], mrecv_sem.at[k], mate)
 
+    def x_first(k, rest):
+        lo, size = (FEW, KEPT - FEW) if rest else (0, FEW)
+        to = device(dx=(1, 3)[k])
+        sem = NZ if rest else 0
+        return remote(
+            xs.at[0, pl.ds(lo, size)], xs.at[0, pl.ds((k + 1) * KEPT + lo, size)], xsend_sem.at[sem, k],
+            xrecv_sem.at[sem, k], to,
+        )
+
     def x_copy(t, k):
         if k == 0:
             src, dst, to = pl.ds(0, KEPT), pl.ds(KEPT, KEPT), device(dx=1)
@@ -108,8 +121,8 @@
             gsend_sem.at[k], grecv_sem.at[k], device(dx=d),
         )
 
-    def d_copy(t):
-        return remote(part.at[1 - core, t], near.at[t], dsend_sem.at[t], drecv_sem.at[t], device(dc=1))
+    def d_copy(u):
+        return remote(part.at[1 - core, u], near.at[u], dsend_sem.at[u], drecv_sem.at[u], device(dc=1))
 
     def a_copy(t, k):
         to = device(dy=(1, 3)[k])
@@ -126,7 +139,7 @@
         )
 
     def z_copy(t):
-        to = device(dz=t + 1)
+        to = device(dz=t // PARTS + 1)
         return (
             remote(zsend.at[t], zrecv.at[t], zsend_sem.at[t, 0], zrecv_sem.at[t, 0], to),
             remote(zscale.at[t], zrscale.at[t], zsend_sem.at[t, 1], zrecv_sem.at[t, 1], to),
@@ -156,37 +169,55 @@
     many = y >= NY // 2
     x_load.wait()
 
+    def block(t, j):
+        return pl.ds(pl.multiple_of((j * NZ + target(t)) * BLOCK, BLOCK), BLOCK)
+
     def gather(t, carry):
         for j in range(NY):
-            at = pl.multiple_of((j * NZ + target(t)) * BLOCK, BLOCK)
             to = slice(j * BLOCK, (j + 1) * BLOCK)
-            xs[t, 0:FEW, to] = xraw[0:FEW, pl.ds(at, BLOCK)]
-            xs[t, FEW + MOVED : KEPT, to] = xraw[FEW + MOVED : KEPT, pl.ds(at, BLOCK)]
-            xmove[t, :, to] = xraw[KEPT:ROWS, pl.ds(at, BLOCK)]
+            xs[t, 0:FEW, to] = xraw[0:FEW, block(t, j)]
+            xs[t, FEW + MOVED : KEPT, to] = xraw[FEW + MOVED : KEPT, block(t, j)]
 
             @pl.when(many)
             def _():
-                xs[t, FEW : FEW + MOVED, to] = xraw[FEW : FEW + MOVED, pl.ds(at, BLOCK)]
+                xs[t, FEW : FEW + MOVED, to] = xraw[FEW : FEW + MOVED, block(t, j)]
 
         return carry
 
-    lax.fori_loop(0, NZ, gather, 0)
+    def hand(t, carry):
+        for j in range(NY):
+            xmove[t, :, j * BLOCK : (j + 1) * BLOCK] = xraw[KEPT:ROWS, block(t, j)]
+        return carry
+
+    @pl.when(many)
+    def _():
+        lax.fori_loop(0, NZ, hand, 0)
+
+    gather(0, 0)
     pl.semaphore_wait(barrier, len(partners))
 
     @pl.when(many)
     def _():
         move(0).start()
+
+    x_first(0, False).start()
+    x_first(1, False).start()
+
+    @pl.when(many)
+    def _():
         move(1).start()
 
+    lax.fori_loop(1, NZ, gather, 0)
     count_send(0)
 
     @pl.when(jnp.logical_not(many))
     def _():
         move(0).wait_recv()
 
-    for t in range(2):
-        x_copy(t, 0).start()
-        x_copy(t, 1).start()
+    x_first(0, True).start()
+    x_first(1, True).start()
+    x_copy(1, 0).start()
+    x_copy(1, 1).start()
 
     own = xraw[...]
     act = lax.dot_general(own, own, (((1,), (1,)), ((), ())), preferred_element_type=F32)
@@ -225,44 +256,68 @@
     for q in range(NX):
         clip(q, 0, FEW)
 
-    for t in range(2):
-        x_copy(t, 0).wait_recv()
-        x_copy(t, 1).wait_recv()
-        x_copy(t, 2).start()
-        x_copy(t, 3).start()
+    for k in range(2):
+        x_first(k, False).wait_recv()
+        x_first(k, True).wait_recv()
+    x_copy(0, 2).start()
+    x_copy(0, 3).start()
 
     @pl.when(jnp.logical_not(many))
     def _():
+        move(1).wait_recv()
+
+    x_copy(2, 0).start()
+    x_copy(2, 1).start()
+    x_copy(1, 0).wait_recv()
+    x_copy(1, 1).wait_recv()
+    x_copy(1, 2).start()
+    x_copy(1, 3).start()
+
+    @pl.when(jnp.logical_not(many))
+    def _():
         move(2).wait_recv()
-        move(1).wait_recv()
 
     for k in range(3):
         g_copy(k).start()
-    x_copy(2, 0).start()
-    x_copy(2, 1).start()
+    x_copy(3, 0).start()
+    x_copy(3, 1).start()
     gs[0:KEPT] = gcut[x, 0:KEPT]
+    fin_send[...] = jnp.zeros((HALF, QUARTER), F32)
+    x_copy(2, 0).wait_recv()
+    x_copy(2, 1).wait_recv()
+    x_copy(2, 2).start()
+    x_copy(2, 3).start()
+    x_copy(4, 0).start()
+    x_copy(4, 1).start()
+    for k in range(3):
+        g_copy(k).wait()
+
+    ahead, behind = lax.rem(y + 1, NY), lax.rem(y + 3, NY)
+    far = lax.rem(y + 2, NY)
+
+    def columns(u):
+        return pl.ds(pl.multiple_of((u % PARTS) * COLS, BLOCK), COLS)
 
     def step(i, carry):
-        @pl.when(i + 2 < NZ)
-        def _():
-            x_copy(i + 2, 0).start()
-            x_copy(i + 2, 1).start()
-
-        @pl.when((i >= 2) & (i < NZ))
-        def _():
-            x_copy(i, 0).wait_recv()
-            x_copy(i, 1).wait_recv()
-            x_copy(i, 2).start()
-            x_copy(i, 3).start()
-
-        @pl.when(i == 1)
-        def _():
-            for k in range(3):
-                g_copy(k).wait()
-
-        @pl.when(i < NZ + 1)
-        def _():
-            t = i - 1
+        begin = i % PARTS == 0
+        now = i // PARTS
+
+        @pl.when(begin & (now >= 2) & (now + 1 < NZ))
+        def _():
+            t = now + 1
+            x_copy(t, 0).wait_recv()
+            x_copy(t, 1).wait_recv()
+            x_copy(t, 2).start()
+            x_copy(t, 3).start()
+
+            @pl.when(t + 2 < NZ)
+            def _():
+                x_copy(t + 2, 0).start()
+                x_copy(t + 2, 1).start()
+
+        @pl.when(begin & (now < NZ))
+        def _():
+            t = now
             x_copy(t, 2).wait_recv()
             x_copy(t, 3).wait_recv()
             for pair in range(NY // 2):
@@ -272,82 +327,103 @@
                 )
                 for k in range(2):
                     for h in range(2):
-                        part[h, t, 2 * pair + k] = tile[k * BLOCK + h * HALF : k * BLOCK + (h + 1) * HALF]
-            d_copy(t).start()
+                        rows = slice(k * BLOCK + h * HALF, k * BLOCK + (h + 1) * HALF)
+                        for n in range(PARTS):
+                            part[h, t * PARTS + n, 2 * pair + k] = tile[rows, n * COLS : (n + 1) * COLS]
+            for n in range(PARTS):
+                d_copy(t * PARTS + n).start()
 
         for stage in range(4):
-            @pl.when(i == 2 * stage + 1)
+            @pl.when(i == 4 * stage + 1)
             def _(stage=stage):
                 value = count_take(stage)
                 tally[0, stage + 1] = value
                 if stage < 3:
                     count_send(stage + 1)
 
-        ahead, behind = lax.rem(y + 1, NY), lax.rem(y + 3, NY)
-        far = lax.rem(y + 2, NY)
-
-        @pl.when((i >= 2) & (i < NZ + 2))
-        def _():
-            t = i - 2
-            d_copy(t).wait_recv()
+        @pl.when((i >= 1) & (i < UNITS + 1))
+        def _():
+            u = i - 1
+            d_copy(u).wait_recv()
             for k in range(2):
                 rows = slice(k * SIDE, (k + 1) * SIDE)
-                code, factor = quantise(part[core, t, far, rows] + near[t, far, rows])
-                asend[t, k] = code
-                ascale[t, k] = factor
-                for copy in a_copy(t, k):
+                code, factor = quantise(part[core, u, far, rows] + near[u, far, rows])
+                asend[u, k] = code
+                ascale[u, k] = factor
+                for copy in a_copy(u, k):
                     copy.start()
 
-        @pl.when((i >= 3) & (i < NZ + 3))
-        def _():
-            t = i - 3
+        @pl.when((i >= 3) & (i < UNITS + 3))
+        def _():
+            u = i - 3
             for k in range(2):
                 to = (ahead, behind)[k]
-                value = part[core, t, to] + near[t, to]
-                for copy in a_copy(t, k):
+                value = part[core, u, to] + near[u, to]
+                for copy in a_copy(u, k):
                     copy.wait_recv()
-                more = restore(arecv[t, k], arscale[t, k])
+                more = restore(arecv[u, k], arscale[u, k])
                 if k == 0:
                     value = jnp.concatenate([value[:SIDE] + more, value[SIDE:]], axis=0)
                 else:
                     value = jnp.concatenate([value[:SIDE], value[SIDE:] + more], axis=0)
                 code, factor = quantise(value)
-                ysend[t, k] = code
-                yscale[t, k] = factor
-                for copy in y_copy(t, k):
+                ysend[u, k] = code
+                yscale[u, k] = factor
+                for copy in y_copy(u, k):
                     copy.start()
 
-        @pl.when(i >= 4)
-        def _():
-            t = i - 4
-            value = part[core, t, y] + near[t, y]
+        @pl.when((i >= 5) & (i < UNITS + 5))
+        def _():
+            u = i - 5
+            value = part[core, u, y] + near[u, y]
             for k in range(2):
-                for copy in y_copy(t, k):
+                for copy in y_copy(u, k):
                     copy.wait_recv()
-                value += restore(yrecv[t, k], yrscale[t, k])
-
-            @pl.when(t < NZ - 1)
+                value += restore(yrecv[u, k], yrscale[u, k])
+
+            @pl.when(u < SENT)
             def _():
                 code, factor = quantise(value)
-                zsend[t] = code
-                zscale[t] = factor
-                for copy in z_copy(t):
+                zsend[u] = code
+                zscale[u] = factor
+                for copy in z_copy(u):
                     copy.start()
 
-            @pl.when(t == NZ - 1)
+            @pl.when(u >= SENT)
             def _():
-                fin_send[...] = value
+                fin_send[:, columns(u)] += value
+
+        @pl.when(i >= 9)
+        def _():
+            u = i - 9
+            for copy in z_copy(u):
+                copy.wait_recv()
+            fin_send[:, columns(u)] += restore(zrecv[u], zrscale[u])
+
+        @pl.when((i >= 8) & (i < UNITS + 6))
+        def _():
+            sent(i - 8)
+
+        @pl.when(begin & (now >= 3))
+        def _():
+            for k in range(4):
+                x_copy(now - 2, k).wait_send()
 
         return carry
 
-    lax.fori_loop(1, NZ + 4, step, 0)
-
-    value = fin_send[...]
-    for t in range(NZ - 1):
-        for copy in z_copy(t):
-            copy.wait_recv()
-        value += restore(zrecv[t], zrscale[t])
-    fin_send[...] = value
+    def sent(u):
+        d_copy(u).wait_send()
+        for k in range(2):
+            for copy in a_copy(u, k) + y_copy(u, k):
+                copy.wait_send()
+
+        @pl.when(u < SENT)
+        def _():
+            for copy in z_copy(u):
+                copy.wait_send()
+
+    lax.fori_loop(0, UNITS + 6, step, 0)
+
     shift = QUARTER - PAD
     mine = pl.ds(pl.multiple_of(core * HALF, HALF), HALF)
     last = remote(
@@ -358,19 +434,12 @@
     full[mine] = fin_send[:, pl.ds(pl.multiple_of(core * shift, BLOCK), PAD)]
     admitted = tally[0, 4, 0:1, 0:1].astype(F32)
 
-    def drain(t, carry):
-        for k in range(4):
-            x_copy(t, k).wait_send()
-        d_copy(t).wait_send()
-        for k in range(2):
-            for copy in a_copy(t, k) + y_copy(t, k):
-                copy.wait_send()
-        return carry
-
-    lax.fori_loop(0, NZ, drain, 0)
-    for t in range(NZ - 1):
-        for copy in z_copy(t):
-            copy.wait_send()
+    for u in (UNITS - 2, UNITS - 1):
+        sent(u)
+    for k in range(2):
+        x_first(k, False).wait_send()
+        x_first(k, True).wait_send()
+        x_copy(0, 2 + k).wait_send()
 
     @pl.when(many)
     def _():
@@ -405,20 +474,20 @@
             pltpu.VMEM((ROWS, width), bf16),
             pltpu.VMEM((NX, ROWS, QUARTER), bf16),
             pltpu.VMEM((NX * KEPT, QUARTER), bf16),
-            pltpu.VMEM((2, NZ, NY, HALF, QUARTER), F32),
-            pltpu.VMEM((NZ, NY, HALF, QUARTER), F32),
-            pltpu.VMEM((NZ, 2, SIDE, QUARTER), i16),
-            pltpu.VMEM((NZ, 2, 1, QUARTER), F32),
-            pltpu.VMEM((NZ, 2, SIDE, QUARTER), i16),
-            pltpu.VMEM((NZ, 2, 1, QUARTER), F32),
-            pltpu.VMEM((NZ, 2, HALF, QUARTER), i16),
-            pltpu.VMEM((NZ, 2, 1, QUARTER), F32),
-            pltpu.VMEM((NZ, 2, HALF, QUARTER), i16),
-            pltpu.VMEM((NZ, 2, 1, QUARTER), F32),
-            pltpu.VMEM((NZ - 1, HALF, QUARTER), i16),
-            pltpu.VMEM((NZ - 1, 1, QUARTER), F32),
-            pltpu.VMEM((NZ - 1, HALF, QUARTER), i16),
-            pltpu.VMEM((NZ - 1, 1, QUARTER), F32),
+            pltpu.VMEM((2, UNITS, NY, HALF, COLS), F32),
+            pltpu.VMEM((UNITS, NY, HALF, COLS), F32),
+            pltpu.VMEM((UNITS, 2, SIDE, COLS), i16),
+            pltpu.VMEM((UNITS, 2, 1, COLS), F32),
+            pltpu.VMEM((UNITS, 2, SIDE, COLS), i16),
+            pltpu.VMEM((UNITS, 2, 1, COLS), F32),
+            pltpu.VMEM((UNITS, 2, HALF, COLS), i16),
+            pltpu.VMEM((UNITS, 2, 1, COLS), F32),
+            pltpu.VMEM((UNITS, 2, HALF, COLS), i16),
+            pltpu.VMEM((UNITS, 2, 1, COLS), F32),
+            pltpu.VMEM((SENT, HALF, COLS), i16),
+            pltpu.VMEM((SENT, 1, COLS), F32),
+            pltpu.VMEM((SENT, HALF, COLS), i16),
+            pltpu.VMEM((SENT, 1, COLS), F32),
             pltpu.VMEM((HALF, QUARTER), F32),
             pltpu.VMEM((BLOCK, PAD), F32),
             pltpu.VMEM((PAD, BLOCK), F32),
@@ -426,18 +495,18 @@
             dma((2,)),
             dma((3,)),
             dma((3,)),
-            dma((NZ, 4)),
-            dma((NZ, 4)),
+            dma((NZ + 1, 4)),
+            dma((NZ + 1, 4)),
             dma((3,)),
             dma((3,)),
-            dma((NZ,)),
-            dma((NZ,)),
-            dma((NZ, 2, 2)),
-            dma((NZ, 2, 2)),
-            dma((NZ, 2, 2)),
-            dma((NZ, 2, 2)),
-            dma((NZ - 1, 2)),
-            dma((NZ - 1, 2)),
+            dma((UNITS,)),
+            dma((UNITS,)),
+            dma((UNITS, 2, 2)),
+            dma((UNITS, 2, 2)),
+            dma((UNITS, 2, 2)),
+            dma((UNITS, 2, 2)),
+            dma((SENT, 2)),
+            dma((SENT, 2)),
             dma,
             dma,
             dma((14,)),

time: 130 us -> 123 us (0.946)
  Pallas kernels: 128 us -> 120 us
    pallas_call x1, Pallas kernels: 128 us -> 120 us  [on_device(): pl.pallas_call(kernel, out_shape=jax.ShapeDtypeStruct(gauss_noise.shape[:...]
where the time goes in v3:
time: 123 us
  Pallas kernels  120 us (98%)
  local copies, waits for them, and re-layouts  1.69 us (1%)
    pallas_call x1, Pallas kernels, on_device(): pl.pallas_call(kernel, out_shape=jax.ShapeDtypeStruct(gauss_noise.shape[:...  120 us

profile of v3, /device:TPU:1, one launch (start us, length us, event | category | flops | bytes accessed | tf_op | source)
XLA Modules:
  0.0 122.6 jit_solution(13473898595263798700)
XLA Ops:
  0.7 120.3 %shard_map.55 = f32[576,128]{1,0:T(8,128)} custom-call(s32[1]{0:T(128)S(6)} %copy.7.count_ref, s32[1,3]{1,0:T(1,128)} %lengths_ref.1, bf16[256,4096]{1,0:T(8,128)(2,1)} %x_hbm.1, bf16[256,4608]{1,0:T(8,128)(2,1)} %g_hbm.1, f32[576,128]{1,0:T(8,128)} %bitcast.3), custom_call_target="tpu_custom_call" | custom-call | flops 10000000000 | bytes 5000000 | tf_op jit(solution)/shard_map/pallas_call | solution.py:459
  120.9 1.7 %copy.8 = f32[128,576]{0,1:T(8,128)} copy(f32[128,576]{0,1:T(8,128)} %bitcast.2) | data formatting | bytes 589824

commit v4 on v2

v4 whole, which is shorter than its diff:
```python
import functools

import jax
import jax.numpy as jnp
from jax import lax
from jax.experimental import pallas as pl
from jax.experimental.pallas import tpu as pltpu
from jax.sharding import PartitionSpec as P

MAXSEQ = 3
CLIP = 360000
MESH = pl.DeviceIdType.MESH
NX, NY, NZ = 4, 4, 8
ROWS = 240
FEW = 160
MOVED = 32
KEPT = ROWS - MOVED
CUT = 112
BLOCK = 128
CHUNK = NY * BLOCK
HALF = BLOCK // 2
SIDE = HALF // 2
QUARTER = 1152
LAST = NZ - 1
ENDING = NZ - 2
ORDER = (2, 1, 3, 0)
TAIL = (((6, 0), (7, 0)), ((6, 1), (6, 2)), ((7, 1), (7, 2)), ((6, 3), (7, 3)))
WIDTH = 576
PAD = 640
F32 = jnp.float32


def quantise(value):
    top = jnp.maximum(jnp.max(jnp.abs(value), axis=0, keepdims=True), 1e-30)
    code = jnp.round(value * (32767.0 / top)).astype(jnp.int32).astype(jnp.int16)
    return code, top * (1.0 / 32767.0)


def restore(code, scale):
    return code.astype(jnp.int32).astype(F32) * scale


def kernel(
    count_ref, lengths_ref, x_hbm, g_hbm, noise_hbm, out_ref,
    xraw, xmove, xs, graw, gcut, gs, noise, part, near,
    asend, ascale, arecv, arscale, ysend, yscale, yrecv, yrscale,
    zsend, zscale, zrecv, zrscale, fin_send, full, turned, tally,
    load_sem, msend_sem, mrecv_sem, xsend_sem, xrecv_sem, gsend_sem, grecv_sem, dsend_sem, drecv_sem,
    asend_sem, arecv_sem, ysend_sem, yrecv_sem, zsend_sem, zrecv_sem,
    fsend_sem, frecv_sem, csend_sem, crecv_sem,
):
    dp = lax.axis_index("dp")
    fs = lax.axis_index("fsdp")
    x, core = fs // 2, fs % 2
    y, z = dp // NZ, dp % NZ
    one = 1 + 2 * core
    two = NX - one

    def device(dx=0, dy=0, dz=0, dc=0):
        return (
            lax.rem(y + dy, NY) * NZ + lax.rem(z + dz, NZ),
            lax.rem(x + dx, NX) * 2 + lax.rem(core + dc, 2),
        )

    partners = (
        [device(dx=d) for d in (1, 2, 3)]
        + [device(dy=d) for d in (1, 2, 3)]
        + [device(dz=d) for d in range(1, NZ)]
        + [device(dc=1)]
    )
    barrier = pltpu.get_barrier_semaphore()
    for partner in partners:
        pl.semaphore_signal(barrier, inc=1, device_id=partner, device_id_type=MESH)

    x_load = pltpu.make_async_copy(x_hbm.at[pl.ds(0, ROWS)], xraw, load_sem.at[0])
    g_load = pltpu.make_async_copy(g_hbm.at[pl.ds(0, ROWS)], graw, load_sem.at[1])
    n_load = pltpu.make_async_copy(noise_hbm, noise, load_sem.at[2])
    x_load.start()
    g_load.start()
    n_load.start()
    tally[0, 0] = jnp.full((8, 128), count_ref[0], jnp.int32)

    def away(t):
        odd = t % 2
        return (1 - odd) * (NZ // 2 - t // 2) + odd * (NZ // 2 + 1 + t // 2)

    def target(t):
        return lax.rem(z + away(t), NZ)

    def remote(src, dst, send, recv, to):
        return pltpu.make_async_remote_copy(
            src_ref=src, dst_ref=dst, send_sem=send, recv_sem=recv, device_id=to, device_id_type=MESH
        )

    mate = device(dy=lax.rem(7 - 2 * y, NY))

    def move(k):
        if k == 2:
            src, dst = gcut.at[:, pl.ds(KEPT, MOVED)], gcut.at[:, pl.ds(FEW, MOVED)]
        else:
            steps = pl.ds(0, 2) if k == 0 else pl.ds(2, NZ - 2)
            src, dst = xmove.at[steps], xs.at[steps, pl.ds(FEW, MOVED)]
        return remote(src, dst, msend_sem.at[k], mrecv_sem.at[k], mate)

    def x_rows(k):
        if k == 0:
            return pl.ds(0, KEPT), pl.ds(KEPT, KEPT), device(dx=one)
        if k == 1:
            return pl.ds(0, KEPT), pl.ds(2 * KEPT, KEPT), device(dx=two)
        if k == 2:
            return pl.ds(KEPT, CUT), pl.ds(3 * KEPT, CUT), device(dx=one)
        return pl.ds(2 * KEPT + CUT, KEPT - CUT), pl.ds(3 * KEPT + CUT, KEPT - CUT), device(dx=two)

    def x_first(k, rest):
        lo, size = (FEW, KEPT - FEW) if rest else (0, FEW)
        sem = NZ + 2 if rest else 0
        return remote(
            xs.at[0, pl.ds(lo, size)], xs.at[0, pl.ds((k + 1) * KEPT + lo, size)], xsend_sem.at[sem, k],
            xrecv_sem.at[sem, k], device(dx=(one, two)[k]),
        )

    def x_copy(t, k):
        src, dst, to = x_rows(k)
        return remote(xs.at[t, src], xs.at[t, dst], xsend_sem.at[t, k], xrecv_sem.at[t, k], to)

    def x_half(h, k):
        src, dst, to = x_rows(k)
        t, cols = ENDING + h // 2, pl.ds((h % 2) * 2 * BLOCK, 2 * BLOCK)
        return remote(
            xs.at[t, src, cols], xs.at[t, dst, cols], xsend_sem.at[ENDING + h, k], xrecv_sem.at[ENDING + h, k], to
        )

    def g_copy(k, rest):
        d = (one, two, 2)[k]
        lo, size = (FEW, KEPT - FEW) if rest else (0, FEW)
        return remote(
            gcut.at[lax.rem(x + d, NX), pl.ds(lo, size)], gs.at[pl.ds((k + 1) * KEPT + lo, size)],
            gsend_sem.at[k, rest], grecv_sem.at[k, rest], device(dx=d),
        )

    def d_piece(t, p):
        return remote(
            part.at[1 - core, t, p], near.at[t, p], dsend_sem.at[t, p], drecv_sem.at[t, p], device(dc=1)
        )

    def d_copy(t, pair):
        two_of = pl.ds(2 * pair, 2)
        return remote(
            part.at[1 - core, t, two_of], near.at[t, two_of], dsend_sem.at[t, pair], drecv_sem.at[t, pair], device(dc=1)
        )

    def a_copy(t, k):
        to = device(dy=(1, 3)[k])
        return (
            remote(asend.at[t, k], arecv.at[t, k], asend_sem.at[t, k, 0], arecv_sem.at[t, k, 0], to),
            remote(ascale.at[t, k], arscale.at[t, k], asend_sem.at[t, k, 1], arecv_sem.at[t, k, 1], to),
        )

    def y_copy(t, k):
        to = device(dy=(1, 3)[k])
        return (
            remote(ysend.at[t, k], yrecv.at[t, k], ysend_sem.at[t, k, 0], yrecv_sem.at[t, k, 0], to),
            remote(yscale.at[t, k], yrscale.at[t, k], ysend_sem.at[t, k, 1], yrecv_sem.at[t, k, 1], to),
        )

    def z_copy(t):
        to = device(dz=away(t))
        return (
            remote(zsend.at[t], zrecv.at[t], zsend_sem.at[t, 0], zrecv_sem.at[t, 0], to),
            remote(zscale.at[t], zrscale.at[t], zsend_sem.at[t, 1], zrecv_sem.at[t, 1], to),
        )

    stages = (("dc", (1,)), ("dx", (1, 2, 3)), ("dy", (1, 2, 3)), ("dz", tuple(range(1, NZ))))
    first = (0, 1, 4, 7, 14)

    def c_copy(stage, i):
        axis, steps = stages[stage]
        slot = first[stage] + i
        return remote(
            tally.at[0, stage], tally.at[1, slot], csend_sem.at[slot], crecv_sem.at[slot], device(**{axis: steps[i]})
        )

    def count_send(stage):
        for i in range(len(stages[stage][1])):
            c_copy(stage, i).start()

    def count_take(stage):
        value = tally[0, stage]
        for i in range(len(stages[stage][1])):
            c_copy(stage, i).wait()
            value = value + tally[1, first[stage] + i]
        return value

    many = y >= NY // 2
    x_load.wait()

    def block(t, j, owner=y):
        if isinstance(t, int) and t >= ENDING:
            t, j = TAIL[2 * (t - ENDING) + j // 2][j % 2]
        return pl.ds(pl.multiple_of((lax.rem(owner + ORDER[j], NY) * NZ + target(t)) * BLOCK, BLOCK), BLOCK)

    def gather(t, carry):
        for j in range(NY):
            to = slice(j * BLOCK, (j + 1) * BLOCK)
            xs[t, 0:FEW, to] = xraw[0:FEW, block(t, j)]
            xs[t, FEW + MOVED : KEPT, to] = xraw[FEW + MOVED : KEPT, block(t, j)]

            @pl.when(many)
            def _():
                xs[t, FEW : FEW + MOVED, to] = xraw[FEW : FEW + MOVED, block(t, j)]

        return carry

    def hand(t, carry):
        for j in range(NY):
            xmove[t, :, j * BLOCK : (j + 1) * BLOCK] = xraw[KEPT:ROWS, block(t, j, NY - 1 - y)]
        return carry

    @pl.when(many)
    def _():
        lax.fori_loop(0, ENDING, hand, 0)
        for t in range(ENDING, NZ):
            hand(t, 0)

    gather(0, 0)
    pl.semaphore_wait(barrier, len(partners))

    @pl.when(many)
    def _():
        move(0).start()

    x_first(0, False).start()
    x_first(1, False).start()

    @pl.when(many)
    def _():
        move(1).start()

    gather(1, 0)
    count_send(0)

    @pl.when(jnp.logical_not(many))
    def _():
        move(0).wait_recv()

    x_first(0, True).start()
    x_first(1, True).start()
    x_copy(1, 0).start()
    x_copy(1, 1).start()

    own = xraw[...]
    act = lax.dot_general(own, own, (((1,), (1,)), ((), ())), preferred_element_type=F32)
    g_load.wait()
    own = graw[...]
    grad = lax.dot_general(own, own, (((1,), (1,)), ((), ())), preferred_element_type=F32)
    product = act * grad
    row = lax.broadcasted_iota(jnp.int32, (ROWS, ROWS), 0)
    col = lax.broadcasted_iota(jnp.int32, (ROWS, ROWS), 1)
    line = lax.broadcasted_iota(jnp.int32, (ROWS, 1), 0)
    scale = jnp.zeros((ROWS, 1), F32)
    start = jnp.int32(0)
    for j in range(MAXSEQ):
        used = jnp.where(j < count_ref[0], lengths_ref[0, j], 0)
        end = start + used
        both = (row >= start) & (row < end) & (col >= start) & (col < end)
        sums = jnp.sum(jnp.where(both, product, 0.0), axis=1, keepdims=True)
        norm_sq = jnp.sum(sums, axis=0, keepdims=True)
        factor = CLIP / jnp.maximum(jnp.sqrt(norm_sq), F32(CLIP))
        scale = jnp.where((line >= start) & (line < end), factor, scale)
        start = end

    def clip(q, lo, hi):
        rows = graw[lo:hi, pl.ds(pl.multiple_of(q * QUARTER, BLOCK), QUARTER)].astype(F32)
        gcut[q, lo:hi] = (scale[lo:hi] * rows).astype(jnp.bfloat16)

    for q in range(NX):
        clip(q, FEW + MOVED, ROWS)

    @pl.when(many)
    def _():
        move(2).start()

    for d in range(NX):
        clip(lax.rem(x + 1 + d, NX), 0, FEW)
    for k in range(3):
        g_copy(k, 0).start()

    @pl.when(many)
    def _():
        for q in range(NX):
            clip(q, FEW, FEW + MOVED)
        for k in range(3):
            g_copy(k, 1).start()

    for k in range(2):
        x_first(k, False).wait_recv()
        x_first(k, True).wait_recv()
    x_copy(0, 2).start()
    x_copy(0, 3).start()

    @pl.when(jnp.logical_not(many))
    def _():
        move(2).wait_recv()
        for k in range(3):
            g_copy(k, 1).start()

    lax.fori_loop(2, ENDING, gather, 0)
    for t in range(ENDING, NZ):
        gather(t, 0)
    gs[0:KEPT] = gcut[x, 0:KEPT]
    fin_send[...] = jnp.zeros((HALF, QUARTER), F32)

    @pl.when(jnp.logical_not(many))
    def _():
        move(1).wait_recv()

    x_copy(1, 0).wait_recv()
    x_copy(1, 1).wait_recv()
    x_copy(1, 2).start()
    x_copy(1, 3).start()
    for k in range(3):
        g_copy(k, 0).wait_recv()
    x_copy(2, 0).start()
    x_copy(2, 1).start()
    for k in range(3):
        g_copy(k, 1).wait_recv()
    x_copy(3, 0).start()
    x_copy(3, 1).start()

    def multiply(t, pair, pieces):
        cols = slice(pair * 2 * BLOCK, (pair + 1) * 2 * BLOCK)
        tile = lax.dot_general(xs[t, :, cols], gs[...], (((0,), (0,)), ((), ())), preferred_element_type=F32)
        for k in range(2):
            for h in range(2):
                part[h, pieces[k][0], pieces[k][1]] = tile[k * BLOCK + h * HALF : k * BLOCK + (h + 1) * HALF]

    def spread(t):
        for k in range(2):
            rows = slice(k * SIDE, (k + 1) * SIDE)
            code, factor = quantise(part[core, t, 0, rows] + near[t, 0, rows])
            asend[t, k] = code
            ascale[t, k] = factor
            for copy in a_copy(t, k):
                copy.start()

    def pass_on(t, k):
        value = part[core, t, 1 + k] + near[t, 1 + k]
        for copy in a_copy(t, k):
            copy.wait_recv()
        more = restore(arecv[t, k], arscale[t, k])
        if k == 0:
            value = jnp.concatenate([value[:SIDE] + more, value[SIDE:]], axis=0)
        else:
            value = jnp.concatenate([value[:SIDE], value[SIDE:] + more], axis=0)
        code, factor = quantise(value)
        ysend[t, k] = code
        yscale[t, k] = factor
        for copy in y_copy(t, k):
            copy.start()

    def collect(t):
        value = part[core, t, 3] + near[t, 3]
        for k in range(2):
            for copy in y_copy(t, k):
                copy.wait_recv()
            value += restore(yrecv[t, k], yrscale[t, k])
        return value

    def deliver(t):
        code, factor = quantise(collect(t))
        zsend[t] = code
        zscale[t] = factor
        for copy in z_copy(t):
            copy.start()

    def accept(t):
        for copy in z_copy(t):
            copy.wait_recv()
        fin_send[...] += restore(zrecv[t], zrscale[t])

    def sent(t):
        for k in range(2):
            for copy in a_copy(t, k) + y_copy(t, k):
                copy.wait_send()

    def product(t):
        x_copy(t, 2).wait_recv()
        x_copy(t, 3).wait_recv()
        for pair in range(2):
            multiply(t, pair, ((t, 2 * pair), (t, 2 * pair + 1)))
            d_copy(t, pair).start()

    def onward(t):
        d_copy(t, 1).wait_recv()
        pass_on(t, 0)
        pass_on(t, 1)

    def step(t, carry):
        @pl.when(t >= 1)
        def _():
            i = t + 1
            x_copy(i, 0).wait_recv()
            x_copy(i, 1).wait_recv()
            x_copy(i, 2).start()
            x_copy(i, 3).start()

            @pl.when(t <= 2)
            def _():
                x_copy(t + 3, 0).start()
                x_copy(t + 3, 1).start()

            @pl.when(t == 3)
            def _():
                for h in range(2):
                    for k in range(2):
                        x_half(h, k).start()

            @pl.when(t == 4)
            def _():
                for k in range(2):
                    x_half(2, k).start()

        product(t)

        for stage in range(4):
            @pl.when(t == stage + 1)
            def _(stage=stage):
                value = count_take(stage)
                tally[0, stage + 1] = value
                if stage < 3:
                    count_send(stage + 1)

        d_copy(t, 0).wait_recv()
        spread(t)

        @pl.when(t >= 1)
        def _():
            onward(t - 1)

        @pl.when(t >= 2)
        def _():
            deliver(t - 2)

        @pl.when(t >= 3)
        def _():
            sent(t - 3)
            for k in range(4):
                x_copy(t - 2, k).wait_send()

        return carry

    lax.fori_loop(0, ENDING - 1, step, 0)

    def forward(h):
        for k in range(2):
            x_half(h, k).wait_recv()
        for k in range(2):
            x_half(h, k + 2).start()

    def produce(h):
        for k in range(2):
            x_half(h, k + 2).wait_recv()
        multiply(ENDING + h // 2, h % 2, TAIL[h])
        for t, p in TAIL[h]:
            d_piece(t, p).start()

    def hand_out(t, p):
        d_piece(t, p).wait_recv()
        if p == 0:
            spread(t)
        elif p < 3:
            pass_on(t, p - 1)

    t = ENDING - 1
    forward(0)
    for k in range(2):
        x_half(3, k).start()
    product(t)
    forward(1)
    d_copy(t, 0).wait_recv()
    spread(t)
    onward(t - 1)
    deliver(t - 2)
    forward(2)
    produce(0)
    onward(t)
    hand_out(6, 0)
    hand_out(7, 0)
    deliver(t - 1)
    produce(1)
    forward(3)
    hand_out(6, 1)
    hand_out(6, 2)
    produce(2)
    deliver(t)
    hand_out(7, 1)
    hand_out(7, 2)
    produce(3)
    hand_out(6, 3)
    deliver(6)
    for i in range(LAST - 1):
        accept(i)
    hand_out(7, 3)
    fin_send[...] += collect(LAST)
    accept(LAST - 1)
    shift = QUARTER - PAD
    mine = pl.ds(pl.multiple_of(core * HALF, HALF), HALF)
    last = remote(
        fin_send.at[:, pl.ds(pl.multiple_of((1 - core) * shift, BLOCK), PAD)], full.at[mine], fsend_sem, frecv_sem,
        device(dc=1),
    )
    last.start()
    full[mine] = fin_send[:, pl.ds(pl.multiple_of(core * shift, BLOCK), PAD)]
    admitted = tally[0, 4, 0:1, 0:1].astype(F32)

    for k in range(4):
        for h in range(4):
            x_half(h, k).wait_send()
        for i in range(ENDING - 3, ENDING):
            x_copy(i, k).wait_send()
    for k in range(2):
        x_first(k, False).wait_send()
        x_first(k, True).wait_send()
        x_copy(0, 2 + k).wait_send()
    for i in range(ENDING):
        for pair in range(2):
            d_copy(i, pair).wait_send()
    for i in range(ENDING, NZ):
        for p in range(4):
            d_piece(i, p).wait_send()
    for i in range(ENDING - 4, NZ):
        sent(i)
    for i in range(LAST):
        for copy in z_copy(i):
            copy.wait_send()

    @pl.when(many)
    def _():
        for k in range(3):
            move(k).wait_send()

    n_load.wait()
    for k in range(3):
        for rest in range(2):
            g_copy(k, rest).wait_send()
    last.wait()
    turned[...] = jnp.transpose(full[...])
    lead = pl.multiple_of(core * (PAD - WIDTH), PAD - WIDTH)
    out_ref[...] = (turned[pl.ds(lead, WIDTH)] + noise[...]) / admitted


def on_device(mixed_heads, out_grads, admit_counts, lengths, gauss_noise):
    dma = pltpu.SemaphoreType.DMA
    bf16, i16 = jnp.bfloat16, jnp.int16
    inner, width = mixed_heads.shape[1], out_grads.shape[1]
    turned = pl.pallas_call(
        kernel,
        out_shape=jax.ShapeDtypeStruct(gauss_noise.shape[::-1], F32),
        in_specs=[
            pl.BlockSpec(memory_space=pltpu.SMEM),
            pl.BlockSpec(memory_space=pltpu.SMEM),
            pl.BlockSpec(memory_space=pl.ANY),
            pl.BlockSpec(memory_space=pl.ANY),
            pl.BlockSpec(memory_space=pl.ANY),
        ],
        out_specs=pl.BlockSpec(memory_space=pltpu.VMEM),
        scratch_shapes=[
            pltpu.VMEM((ROWS, inner), bf16),
            pltpu.VMEM((NZ, MOVED, CHUNK), bf16),
            pltpu.VMEM((NZ, NX * KEPT, CHUNK), bf16),
            pltpu.VMEM((ROWS, width), bf16),
            pltpu.VMEM((NX, ROWS, QUARTER), bf16),
            pltpu.VMEM((NX * KEPT, QUARTER), bf16),
            pltpu.VMEM(gauss_noise.shape[::-1], F32),
            pltpu.VMEM((2, NZ, NY, HALF, QUARTER), F32),
            pltpu.VMEM((NZ, NY, HALF, QUARTER), F32),
            pltpu.VMEM((NZ, 2, SIDE, QUARTER), i16),
            pltpu.VMEM((NZ, 2, 1, QUARTER), F32),
            pltpu.VMEM((NZ, 2, SIDE, QUARTER), i16),
            pltpu.VMEM((NZ, 2, 1, QUARTER), F32),
            pltpu.VMEM((NZ, 2, HALF, QUARTER), i16),
            pltpu.VMEM((NZ, 2, 1, QUARTER), F32),
            pltpu.VMEM((NZ, 2, HALF, QUARTER), i16),
            pltpu.VMEM((NZ, 2, 1, QUARTER), F32),
            pltpu.VMEM((LAST, HALF, QUARTER), i16),
            pltpu.VMEM((LAST, 1, QUARTER), F32),
            pltpu.VMEM((LAST, HALF, QUARTER), i16),
            pltpu.VMEM((LAST, 1, QUARTER), F32),
            pltpu.VMEM((HALF, QUARTER), F32),
            pltpu.VMEM((BLOCK, PAD), F32),
            pltpu.VMEM((PAD, BLOCK), F32),
            pltpu.VMEM((2, 14, 8, 128), jnp.int32),
            dma((3,)),
            dma((3,)),
            dma((3,)),
            dma((NZ + 3, 4)),
            dma((NZ + 3, 4)),
            dma((3, 2)),
            dma((3, 2)),
            dma((NZ, 4)),
            dma((NZ, 4)),
            dma((NZ, 2, 2)),
            dma((NZ, 2, 2)),
            dma((NZ, 2, 2)),
            dma((NZ, 2, 2)),
            dma((LAST, 2)),
            dma((LAST, 2)),
            dma,
            dma,
            dma((14,)),
            dma((14,)),
        ],
        compiler_params=pltpu.CompilerParams(
            collective_id=0, has_side_effects=True, vmem_limit_bytes=63 * 1024 * 1024
        ),
        cost_estimate=pl.CostEstimate(flops=10**10, bytes_accessed=5 * 10**6, transcendentals=0),
    )(admit_counts, lengths, mixed_heads, out_grads, gauss_noise.T)
    return turned.T


def solution(mesh):
    in_specs = (
        P(("dp", "fsdp"), None),
        P(("dp", "fsdp"), None),
        P(("dp", "fsdp")),
        P(("dp", "fsdp"), None),
        P("dp", "fsdp"),
    )
    return jax.shard_map(
        on_device, mesh=mesh, in_specs=in_specs, out_specs=P("dp", "fsdp"), check_vma=False
    )
```

time: 130 us -> 115 us (0.88)
  Pallas kernels: 128 us -> 113 us
    pallas_call x1, Pallas kernels: 128 us -> 113 us  [on_device(): pl.pallas_call(kernel, out_shape=jax.ShapeDtypeStruct(gauss_noise.shape[:...]
where the time goes in v4:
time: 115 us
  Pallas kernels  113 us (98%)
  local copies, waits for them, and re-layouts  1.69 us (1%)
    pallas_call x1, Pallas kernels, on_device(): pl.pallas_call(kernel, out_shape=jax.ShapeDtypeStruct(gauss_noise.shape[:...  113 us

profile of v4, /device:TPU:1, one launch (start us, length us, event | category | flops | bytes accessed | tf_op | source)
XLA Modules:
  0.0 115.3 jit_solution(15057911096057669181)
XLA Ops:
  0.7 113.0 %shard_map.55 = f32[576,128]{1,0:T(8,128)} custom-call(s32[1]{0:T(128)S(6)} %copy.7.count_ref, s32[1,3]{1,0:T(1,128)} %lengths_ref.1, bf16[256,4096]{1,0:T(8,128)(2,1)} %x_hbm.1, bf16[256,4608]{1,0:T(8,128)(2,1)} %g_hbm.1, f32[576,128]{1,0:T(8,128)} %bitcast.3), custom_call_target="tpu_custom_call" | custom-call | flops 10000000000 | bytes 5000000 | tf_op jit(solution)/shard_map/pallas_call | solution.py:556
  113.6 1.7 %copy.8 = f32[128,576]{0,1:T(8,128)} copy(f32[128,576]{0,1:T(8,128)} %bitcast.2) | data formatting | bytes 589824

commit v5 on v4

--- a/solution.py
+++ b/solution.py
@@ -433,13 +433,13 @@
         d_copy(t, 0).wait_recv()
         spread(t)
 
+        @pl.when(t >= 2)
+        def _():
+            deliver(t - 2)
+
         @pl.when(t >= 1)
         def _():
             onward(t - 1)
-
-        @pl.when(t >= 2)
-        def _():
-            deliver(t - 2)
 
         @pl.when(t >= 3)
         def _():
@@ -498,21 +498,8 @@
     produce(3)
     hand_out(6, 3)
     deliver(6)
-    for i in range(LAST - 1):
+    for i in range(LAST - 2):
         accept(i)
-    hand_out(7, 3)
-    fin_send[...] += collect(LAST)
-    accept(LAST - 1)
-    shift = QUARTER - PAD
-    mine = pl.ds(pl.multiple_of(core * HALF, HALF), HALF)
-    last = remote(
-        fin_send.at[:, pl.ds(pl.multiple_of((1 - core) * shift, BLOCK), PAD)], full.at[mine], fsend_sem, frecv_sem,
-        device(dc=1),
-    )
-    last.start()
-    full[mine] = fin_send[:, pl.ds(pl.multiple_of(core * shift, BLOCK), PAD)]
-    admitted = tally[0, 4, 0:1, 0:1].astype(F32)
-
     for k in range(4):
         for h in range(4):
             x_half(h, k).wait_send()
@@ -525,24 +512,42 @@
     for i in range(ENDING):
         for pair in range(2):
             d_copy(i, pair).wait_send()
-    for i in range(ENDING, NZ):
-        for p in range(4):
-            d_piece(i, p).wait_send()
-    for i in range(ENDING - 4, NZ):
+    for p in range(4):
+        d_piece(ENDING, p).wait_send()
+    for i in range(ENDING - 4, LAST):
         sent(i)
-    for i in range(LAST):
+    for i in range(LAST - 1):
         for copy in z_copy(i):
             copy.wait_send()
-
-    @pl.when(many)
-    def _():
-        for k in range(3):
-            move(k).wait_send()
-
-    n_load.wait()
     for k in range(3):
         for rest in range(2):
             g_copy(k, rest).wait_send()
+
+    @pl.when(many)
+    def _():
+        for k in range(3):
+            move(k).wait_send()
+
+    hand_out(7, 3)
+    accept(LAST - 2)
+    fin_send[...] += collect(LAST)
+    accept(LAST - 1)
+    shift = QUARTER - PAD
+    mine = pl.ds(pl.multiple_of(core * HALF, HALF), HALF)
+    last = remote(
+        fin_send.at[:, pl.ds(pl.multiple_of((1 - core) * shift, BLOCK), PAD)], full.at[mine], fsend_sem, frecv_sem,
+        device(dc=1),
+    )
+    last.start()
+    full[mine] = fin_send[:, pl.ds(pl.multiple_of(core * shift, BLOCK), PAD)]
+    admitted = tally[0, 4, 0:1, 0:1].astype(F32)
+
+    for copy in z_copy(LAST - 1):
+        copy.wait_send()
+    sent(LAST)
+    for p in range(4):
+        d_piece(LAST, p).wait_send()
+    n_load.wait()
     last.wait()
     turned[...] = jnp.transpose(full[...])
     lead = pl.multiple_of(core * (PAD - WIDTH), PAD - WIDTH)

time: 115 us -> 115 us (level)
  no operation moved by 1% of the time
where the time goes in v5:
time: 115 us
  Pallas kernels  113 us (98%)
  local copies, waits for them, and re-layouts  1.69 us (1%)
    pallas_call x1, Pallas kernels, on_device(): pl.pallas_call(kernel, out_shape=jax.ShapeDtypeStruct(gauss_noise.shape[:...  113 us

profile of v5, /device:TPU:1, one launch (start us, length us, event | category | flops | bytes accessed | tf_op | source)
XLA Modules:
  0.0 115.3 jit_solution(3333882686684868508)
XLA Ops:
  0.7 113.0 %shard_map.55 = f32[576,128]{1,0:T(8,128)} custom-call(s32[1]{0:T(128)S(6)} %copy.7.count_ref, s32[1,3]{1,0:T(1,128)} %lengths_ref.1, bf16[256,4096]{1,0:T(8,128)(2,1)} %x_hbm.1, bf16[256,4608]{1,0:T(8,128)(2,1)} %g_hbm.1, f32[576,128]{1,0:T(8,128)} %bitcast.3), custom_call_target="tpu_custom_call" | custom-call | flops 10000000000 | bytes 5000000 | tf_op jit(solution)/shard_map/pallas_call | solution.py:561
  113.6 1.7 %copy.8 = f32[128,576]{0,1:T(8,128)} copy(f32[128,576]{0,1:T(8,128)} %bitcast.2) | data formatting | bytes 589824
